TPU v7x, 32 devices: a whole 2x2x4 slice. The times are simulated.
32 devices in a mesh: grp: 2 (over y), samp: 4 (over z), term: 4 (over x, core).
Axes of the slice: x: 2, y: 2, z: 4, core: 2. Of those that a mesh axis runs over, the one named last changes fastest.
Arguments:
- blocks: float32 [4, 4, 16, 8, 128, 128], P('samp', 'term', 'grp'), parts along dimension 2, may hold values from -0.09375 to 0.09375
- term_index: int32 [4, 4, 16, 8], P('samp', 'term', 'grp'), parts along dimension 2, may hold values from 0 to 63, as said below
- degrees: int32 [256], P('term'), may hold values from 0 to 5, as said below
- targets: float32 [64, 4096], P('grp', 'samp'), parts along dimension 0, may hold values from -6 to 6
Outputs:
- solution: float32 [64, 32768], P('grp', 'term'), parts along dimension 0
- residual: float32 [64, 4096], P('grp', 'samp'), parts along dimension 0
There are 2 independent parts, one for each index of `grp`. A program takes and returns all parts, laid end to end along the dimension named above; an argument that names none is the same for every part. Nothing has to cross between parts.
Inputs may be any that keep to these rules, and one draw needn't show every extreme that they name: `term_index`: each row block holds the gradient rows of one of 40 inputs; on each term device the row blocks of input k touch the 8 term blocks (k * 8 + c + [0, 8)) modulo 64, with c fixed for that term device; so in each row block the indices are distinct. Basis blocks are ordered by total degree: degrees never fall by more than one from a block to a later one.
All inputs are finite; a program needn't handle non-finite values.
Results may differ from a plain program's by a relative error of at most 0.0001.
Values sent between devices are 32-bit elements; how exact they have to be, the bound alone decides.
A program may use at most 64 MiB of HBM per device.

v0:
```python
import jax
import jax.numpy as jnp
from jax import lax
from jax.sharding import PartitionSpec as P

ITERS = 2


def reduce_adjoint(partial_terms):
    return lax.psum(partial_terms, "samp")


def grad_norm_of(grad):
    local_sq = jnp.sum(grad * grad, axis=1)
    return lax.psum(local_sq, "term")


def damped_total(damped_sq):
    return lax.psum(damped_sq, "term")


def local(blocks, term_index, degrees, targets):
    design = blocks[0, 0]
    pattern = term_index[0, 0]
    row_blocks, touched, width, _ = design.shape
    term_blocks = degrees.shape[0]
    num_out = targets.shape[0]
    onehot = (pattern[:, :, None] == jnp.arange(term_blocks, dtype=jnp.int32)).astype(jnp.float32)
    damping = jnp.repeat(0.4 * (1.0 + degrees.astype(jnp.float32)), width)

    def adjoint_part(residual):
        shaped = residual.reshape(num_out, row_blocks, width)
        partial_terms = jnp.einsum(
            "qrx,rnxt->qrnt", shaped, design, precision=lax.Precision.HIGHEST
        )
        summed = jnp.einsum("qrnt,rnb->qbt", partial_terms, onehot, precision=lax.Precision.HIGHEST)
        return summed.reshape(num_out, term_blocks * width)

    residual = targets
    grad = reduce_adjoint(adjoint_part(residual))
    solution = jnp.zeros_like(grad)
    direction = grad
    grad_sq = grad_norm_of(grad)
    for step in range(ITERS):
        forward_shaped = direction.reshape(num_out, term_blocks, width)
        picked = jnp.einsum(
            "qbt,rnb->qrnt", forward_shaped, onehot, precision=lax.Precision.HIGHEST
        )
        image_part = jnp.einsum("qrnt,rnxt->qrx", picked, design, precision=lax.Precision.HIGHEST)
        image = lax.psum(image_part.reshape(num_out, row_blocks * width), "term")
        damped = damping * direction
        image_sq = jnp.sum(image * image, axis=1)
        own_sq = jnp.sum(damped * damped, axis=1)
        curv_sq = lax.psum(image_sq, "samp") + damped_total(own_sq)
        step_size = (grad_sq / curv_sq)[:, None]
        solution = solution + step_size * direction
        residual = residual - step_size * image
        if step + 1 < ITERS:
            grad = reduce_adjoint(adjoint_part(residual)) - damping * damping * solution
            new_sq = grad_norm_of(grad)
            direction = grad + (new_sq / grad_sq)[:, None] * direction
            grad_sq = new_sq
    return (solution, residual)


def solution(mesh):
    placed = (
        P("samp", "term", "grp", None, None, None),
        P("samp", "term", "grp", None),
        P("term"),
        P("grp", "samp"),
    )
    return jax.shard_map(
        local,
        mesh=mesh,
        in_specs=placed,
        out_specs=(P("grp", "term"), P("grp", "samp")),
        check_vma=False,
    )
```

profile of v0, /device:TPU:0, one launch (start us, length us, event | category | flops | bytes accessed | tf_op | source)
XLA Modules:
  0.0 247.0 jit_solution(1756576326322849308)
XLA Ops:
  7.2 0.0 all-reduce.6.cloned.1.call-start
  7.2 0.8 copy.7
  8.0 0.9 copy.23
  8.9 0.0 copy-start.6
  8.9 4.0 %fusion.6 = f32[8,8,128,32]{2,3,1,0:T(8,128)S(1)} fusion(f32[1,1,8,8,128,128]{5,4,3,2,1,0:T(8,128)} %param.4, f32[32,8,128,1]{2,1,0,3:T(8,128)S(1)} %bitcast.103), kind=kOutput, calls=%fused_computation.6 | convolution fusion | flops 402653184 | bytes 5373952 | tf_op jit(solution)/shard_map/qrx,rnxt->qrnt/dot_general | solution.py:33
  13.0 1.3 fusion.18
  14.3 1.6 copy.54
  15.9 0.0 all-reduce.6.cloned.1.call-update
  15.9 0.0 all-reduce.8.cloned.1.call-start
  16.0 0.0 copy-done.6
  16.0 0.1 broadcast_bitcast_fusion
  16.1 54.5 %all-reduce.6.cloned.1.call-done = f32[32,8192]{1,0:T(8,128)} async-done(((f32[32,8192]{1,0:T(8,128)}), f32[32,8192]{1,0:T(8,128)}) %all-reduce.6.cloned.1.call-update) | async-done | bytes 1048592 | tf_op jit(solution)/shard_map/psum | solution.py:10
  70.6 0.0 copy-start
  70.6 1.6 copy.25
  72.1 0.0 copy-start.2
  72.2 0.0 copy-start.4
  72.2 0.7 fusion.32
  72.8 0.3 copy-done
  73.1 4.0 %fusion.8 = f32[8,4,8,128]{3,2,1,0:T(8,128)S(1)} fusion(f32[1,1,8,8,128,128]{5,4,3,2,1,0:T(8,128)S(1)} %copy-done, f32[8,8,32,128]{3,0,2,1:T(8,128)S(1)} %fusion.32), kind=kOutput, calls=%fused_computation.8 | convolution fusion | flops 402653184 | bytes 5373952 | tf_op jit(solution)/shard_map/qrnt,rnxt->qrx/dot_general | solution.py:49
  77.1 0.7 copy.56
  77.8 0.0 all-reduce.8.cloned.1.call-update
  77.8 0.0 all-reduce.10.cloned.1.call-start
  77.9 0.0 copy-done.2
  77.9 0.3 multiply_reduce_fusion.2
  78.2 6.8 %all-reduce = (f32[32]{0:T(128)S(1)}, f32[32]{0:T(128)S(1)}) all-reduce(f32[32]{0:T(128)S(1)} %get-tuple-element.3, f32[32]{0:T(128)S(1)} %get-tuple-element.2), channel_id=1, replica_groups=mesh['grp'=2,'samp'=4,'term'=4] {'term'}, use_global_device_ids=true, to_apply=%region_2.0 | all-reduce | flops 64 | bytes 512 | tf_op jit(solution)/shard_map/psum | solution.py:15
  85.0 23.7 %all-reduce.8.cloned.1.call-done = f32[32,1024]{1,0:T(8,128)} async-done(((f32[32,1024]{1,0:T(8,128)}), f32[32,1024]{1,0:T(8,128)}) %all-reduce.8.cloned.1.call-update) | async-done | bytes 131088 | tf_op jit(solution)/shard_map/psum | solution.py:50
  108.8 1.0 multiply_reduce_fusion.5
  109.8 11.7 %psum.73 = f32[32]{0:T(128)S(1)} all-reduce(f32[32]{0:T(128)S(1)} %multiply_reduce_fusion.5), channel_id=1, replica_groups=mesh['grp'=2,'samp'=4,'term'=4] {'samp'}, use_global_device_ids=true, to_apply=%region_5.0 | all-reduce | flops 32 | bytes 256 | tf_op jit(solution)/shard_map/psum | solution.py:54
  121.5 0.0 copy-done.4
  121.5 1.0 fusion.34
  122.5 4.0 %fusion.2 = f32[8,32,8,128]{3,1,2,0:T(8,128)S(1)} fusion(f32[1,1,8,8,128,128]{5,4,3,2,1,0:T(8,128)} %param.4, f32[32,8,128,1]{2,1,0,3:T(8,128)S(1)} %bitcast.102), kind=kOutput, calls=%fused_computation.2 | convolution fusion | flops 402653184 | bytes 5373952 | tf_op jit(solution)/shard_map/qrx,rnxt->qrnt/dot_general | solution.py:33
  126.6 1.3 fusion.15
  127.9 1.6 copy.53
  129.5 0.0 all-reduce.10.cloned.1.call-update
  129.5 0.0 all-reduce.12.cloned.1.call-start
  129.6 0.1 bitcast_multiply_fusion
  129.6 49.1 %all-reduce.10.cloned.1.call-done = f32[32,8192]{1,0:T(8,128)} async-done(((f32[32,8192]{1,0:T(8,128)}), f32[32,8192]{1,0:T(8,128)}) %all-reduce.10.cloned.1.call-update) | async-done | bytes 1048592 | tf_op jit(solution)/shard_map/psum | solution.py:10
  178.7 1.6 multiply_reduce_fusion.1
  180.3 7.0 %psum.76 = f32[32]{0:T(128)S(1)} all-reduce(f32[32]{0:T(128)S(1)} %multiply_reduce_fusion.1), channel_id=1, replica_groups=mesh['grp'=2,'samp'=4,'term'=4] {'term'}, use_global_device_ids=true, to_apply=%region_10.0 | all-reduce | flops 32 | bytes 256 | tf_op jit(solution)/shard_map/psum | solution.py:15
  187.3 0.0 copy-start.1
  187.3 1.8 multiply_reduce_fusion
  189.1 0.2 copy.28
  189.3 0.0 copy-start.3
  189.3 0.7 fusion.30
  190.0 0.0 copy-done.1
  190.0 0.0 copy-start.5
  190.0 4.0 %fusion.11 = f32[8,4,8,128]{3,2,1,0:T(8,128)S(1)} fusion(f32[1,1,8,8,128,128]{5,4,3,2,1,0:T(8,128)S(1)} %copy-done.1, f32[8,8,32,128]{3,0,2,1:T(8,128)S(1)} %fusion.30), kind=kOutput, calls=%fused_computation.9 | convolution fusion | flops 402653184 | bytes 5373952 | tf_op jit(solution)/shard_map/qrnt,rnxt->qrx/dot_general | solution.py:49
  194.1 0.7 copy.55
  194.7 0.0 all-reduce.12.cloned.1.call-update
  194.8 5.9 %psum.79 = f32[32]{0:T(128)S(1)} all-reduce(f32[32]{0:T(128)S(1)} %get-tuple-element.6), channel_id=1, replica_groups=mesh['grp'=2,'samp'=4,'term'=4] {'term'}, use_global_device_ids=true, to_apply=%region_15.0 | all-reduce | flops 32 | bytes 256 | tf_op jit(solution)/shard_map/psum | solution.py:19
  200.7 24.1 %all-reduce.12.cloned.1.call-done = f32[32,1024]{1,0:T(8,128)} async-done(((f32[32,1024]{1,0:T(8,128)}), f32[32,1024]{1,0:T(8,128)}) %all-reduce.12.cloned.1.call-update) | async-done | bytes 131088 | tf_op jit(solution)/shard_map/psum | solution.py:50
  224.8 1.0 multiply_reduce_fusion.4
  225.8 11.7 %psum.78 = f32[32]{0:T(128)S(1)} all-reduce(f32[32]{0:T(128)S(1)} %multiply_reduce_fusion.4), channel_id=1, replica_groups=mesh['grp'=2,'samp'=4,'term'=4] {'samp'}, use_global_device_ids=true, to_apply=%region_13.0 | all-reduce | flops 32 | bytes 256 | tf_op jit(solution)/shard_map/psum | solution.py:54
  237.5 0.0 copy-done.3
  237.5 1.3 multiply_add_fusion
  238.8 0.0 copy-done.5
  238.8 1.6 multiply_subtract_fusion.1
  (5 shorter events, 0.1 us)
Async XLA Ops:
  7.2 63.4 %all-reduce.6.cloned.1.call-start = ((), (), s32[]{:S(2)}) async-start(), calls=%async_computation | async-start | bytes 2097152 | tf_op jit(solution)/shard_map/psum | solution.py:10
  8.9 7.1 %copy-start.6 = (s32[64]{0:T(128)S(1)}, s32[64]{0:T(128)}, u32[]{:S(2)}) copy-start(s32[64]{0:T(128)} %param.6) | copy-start | bytes 772
  15.9 92.9 %all-reduce.8.cloned.1.call-start = ((), (), s32[]{:S(2)}) async-start(), calls=%async_computation.1 | async-start | bytes 262144 | tf_op jit(solution)/shard_map/psum | solution.py:50
  70.6 2.5 %copy-start = (f32[1,1,8,8,128,128]{5,4,3,2,1,0:T(8,128)S(1)}, f32[1,1,8,8,128,128]{5,4,3,2,1,0:T(8,128)}, u32[]{:S(2)}) copy-start(f32[1,1,8,8,128,128]{5,4,3,2,1,0:T(8,128)} %param.4) | copy-start | bytes 12582916
  72.1 5.7 %copy-start.2 = (f32[32,8192]{1,0:T(8,128)S(1)}, f32[32,8192]{1,0:T(8,128)}, u32[]{:S(2)}) copy-start(f32[32,8192]{1,0:T(8,128)} %all-reduce.6.cloned.1.call-done) | copy-start | bytes 3145732
  72.2 49.3 %copy-start.4 = (f32[32,1024]{1,0:T(8,128)S(1)}, f32[32,1024]{1,0:T(8,128)}, u32[]{:S(2)}) copy-start(f32[32,1024]{1,0:T(8,128)} %param.7) | copy-start | bytes 393220
  77.8 100.9 %all-reduce.10.cloned.1.call-start = ((), (), s32[]{:S(2)}) async-start(), calls=%async_computation.2 | async-start | bytes 2097152 | tf_op jit(solution)/shard_map/psum | solution.py:10
  129.5 95.3 %all-reduce.12.cloned.1.call-start = ((), (), s32[]{:S(2)}) async-start(), calls=%async_computation.3 | async-start | bytes 262144 | tf_op jit(solution)/shard_map/psum | solution.py:50
  187.3 2.7 %copy-start.1 = (f32[1,1,8,8,128,128]{5,4,3,2,1,0:T(8,128)S(1)}, f32[1,1,8,8,128,128]{5,4,3,2,1,0:T(8,128)}, u32[]{:S(2)}) copy-start(f32[1,1,8,8,128,128]{5,4,3,2,1,0:T(8,128)} %param.4) | copy-start | bytes 12582916
  189.3 48.2 %copy-start.3 = (f32[32,8192]{1,0:T(8,128)S(1)}, f32[32,8192]{1,0:T(8,128)}, u32[]{:S(2)}) copy-start(f32[32,8192]{1,0:T(8,128)} %all-reduce.10.cloned.1.call-done) | copy-start | bytes 3145732
  190.0 48.8 %copy-start.5 = (f32[32,1024]{1,0:T(8,128)S(1)}, f32[32,1024]{1,0:T(8,128)}, u32[]{:S(2)}) copy-start(f32[32,1024]{1,0:T(8,128)} %all-reduce.8.cloned.1.call-done) | copy-start | bytes 393220
Sparse Core Ops, SparseCore 0:
  16.0 54.5 all-reduce.5
  78.0 30.7 all-reduce.7
  129.6 49.0 all-reduce.9
  194.9 29.8 all-reduce.11
where the time goes:
time: 247 us
  waiting for transfers between devices  152 us (62%)
  blocking collectives  43.2 us (17%)
  matrix products  20.1 us (8%)
  between operations  13.9 us (6%)
  other arithmetic  9.76 us (4%)
  local copies, waits for them, and re-layouts  8.33 us (3%)
    psum x2, waiting for transfers between devices, reduce_adjoint(): return lax.psum(partial_terms, 'samp')  104 us
    psum x2, waiting for transfers between devices, local(): image = lax.psum(image_part.reshape(num_out, row_blocks * width), 'term')  47.8 us
    psum x2, blocking collectives, local(): curv_sq = lax.psum(image_sq, 'samp') + damped_total(own_sq)  23.4 us
    psum x2, blocking collectives, grad_norm_of(): return lax.psum(local_sq, 'term')  13.9 us
    dot_general x2, matrix products, local(): jnp.einsum('qrnt,rnxt->qrx', picked, design, precision=lax.Precision.HIGH...  8.09 us
    dot_general x2, matrix products, adjoint_part(): jnp.einsum('qrx,rnxt->qrnt', shaped, design, precision=lax.Precision.HIGH...  8.07 us
    unnamed x20, local copies, waits for them, and re-layouts  6.15 us
    psum x1, blocking collectives, damped_total(): return lax.psum(damped_sq, 'term')  5.94 us
  transfers between devices with their start and end apart: 4, of which 4 were waited for; matrix products, arithmetic and copies ran while one was open for 0% of the time, Pallas kernels for 0%

commit v1 on v0

v1 whole, which is shorter than its diff:
```python
import functools

import jax
import jax.numpy as jnp
from jax import lax
from jax.experimental import pallas as pl
from jax.experimental.pallas import tpu as pltpu
from jax.sharding import PartitionSpec as P

MESH = pl.DeviceIdType.MESH
F32 = jnp.float32
BF16 = jnp.bfloat16


def split(x):
    hi = x.astype(BF16)
    return hi, (x - hi.astype(F32)).astype(BF16)


def lane_sum(x):
    return jnp.sum(x, axis=1, keepdims=True)


def kernel(
    n_samp, n_term, chunks,
    tab, deg, a_ref, t_ref,
    sol_ref, res_ref,
    ahi, alo, part, acc0, acc1, rx0, rx1, d0, w1, g1,
    img0, img1, msg0, msg1, trx0, trx1, sr0, sr1, sq0, sq1,
    in_send, out_send, chain_recv, t_send, t_recv, s_send, s_recv,
):
    rows, touched, width = a_ref.shape[2], a_ref.shape[3], a_ref.shape[4]
    num_out = t_ref.shape[0]
    terms = deg.shape[0]
    size = terms // chunks
    half = n_samp // 2
    rounds = n_term.bit_length() - 1
    me = lax.axis_index("samp")
    tm = lax.axis_index("term")

    low = me < half
    inner = jnp.where(low, me + 1, me - 1)
    is_mid = jnp.logical_or(me == half - 1, me == half)
    has_outer = jnp.logical_and(me > 0, me < n_samp - 1)
    outer = jnp.where(low, jnp.maximum(me - 1, 0), jnp.minimum(me + 1, n_samp - 1))
    slot_at_inner = jnp.where(is_mid, 1, 0)

    def peer_of(off):
        return lax.rem(me + off, n_samp)

    def partner_of(k):
        step = 2 ** k
        return tm + (1 - 2 * lax.rem(tm // step, 2)) * step

    barrier = pltpu.get_barrier_semaphore()

    @pl.loop(1, n_samp)
    def _(off):
        pl.semaphore_signal(barrier, inc=1, device_id={"samp": peer_of(off)}, device_id_type=MESH)

    for k in range(rounds):
        pl.semaphore_signal(barrier, inc=1, device_id={"term": partner_of(k)}, device_id_type=MESH)

    def adjoint(load, first):
        @pl.loop(0, rows)
        def _(r):
            if first:
                for n in range(touched):
                    hi, lo = split(a_ref[0, 0, r, n])
                    ahi[r, :, n * width:(n + 1) * width] = hi
                    alo[r, :, n * width:(n + 1) * width] = lo
                part[r * (touched + 1) + touched] = jnp.zeros((num_out, width), F32)
            hi, lo = split(load(r))
            both = jnp.concatenate([hi, lo], axis=0)
            for n in range(touched):
                cols = slice(n * width, (n + 1) * width)
                p = jnp.dot(both, ahi[r, :, cols], preferred_element_type=F32)
                q = jnp.dot(hi, alo[r, :, cols], preferred_element_type=F32)
                part[r * (touched + 1) + n] = p[:num_out] + p[num_out:] + q

    def forward(src, dst):
        @pl.loop(0, rows)
        def _(r):
            x = jnp.concatenate([src[tab[r, terms + n]] for n in range(touched)], axis=1)
            hi, lo = split(x)
            both = jnp.concatenate([hi, lo], axis=0)
            dims = (((1,), (1,)), ((), ()))
            p = lax.dot_general(both, ahi[r], dims, preferred_element_type=F32)
            q = lax.dot_general(hi, alo[r], dims, preferred_element_type=F32)
            dst[0, r] = p[:num_out] + p[num_out:] + q

    def span(c):
        return pl.ds(c * size, size)

    def to_inner(k, acc, rx, c):
        return pltpu.make_async_remote_copy(
            src_ref=acc.at[span(c)], dst_ref=rx.at[slot_at_inner, span(c)],
            send_sem=in_send.at[k, c], recv_sem=chain_recv.at[k, slot_at_inner, c],
            device_id={"samp": inner}, device_id_type=MESH,
        )

    def to_outer(k, d, rx, c):
        return pltpu.make_async_remote_copy(
            src_ref=d.at[span(c)], dst_ref=rx.at[1, span(c)],
            send_sem=out_send.at[k, c], recv_sem=chain_recv.at[k, 1, c],
            device_id={"samp": outer}, device_id_type=MESH,
        )

    def arrived(k, rx, slot, c):
        pltpu.make_async_remote_copy(
            src_ref=rx.at[slot, span(c)], dst_ref=rx.at[slot, span(c)],
            send_sem=in_send.at[k, c], recv_sem=chain_recv.at[k, slot, c],
            device_id={"samp": inner}, device_id_type=MESH,
        ).wait_recv()

    def chain(k, acc, rx, d, visit, carry):
        def inbound(c):
            @pl.loop(0, size)
            def _(i):
                b = c * size + i
                total = part[tab[0, b]]
                for r in range(1, rows):
                    total = total + part[tab[r, b]]
                acc[b] = total

            @pl.when(has_outer)
            def _():
                arrived(k, rx, 0, c)
                acc[span(c)] += rx[0, span(c)]

            to_inner(k, acc, rx, c).start()

        def outbound(c, carry):
            arrived(k, rx, 1, c)

            def one(i, carry):
                b = c * size + i
                got = rx[1, b]
                v = jnp.where(is_mid, got + acc[b], got)
                d[b] = v
                return visit(b, v, carry)

            carry = lax.fori_loop(0, size, one, carry)

            @pl.when(has_outer)
            def _():
                to_outer(k, d, rx, c).start()

            return carry

        inbound(0)

        def step(c, carry):
            inbound(c)
            return outbound(c - 1, carry)

        carry = lax.fori_loop(1, chunks, step, carry)
        return outbound(chunks - 1, carry)

    def term_copy(s, msg, trx, k):
        return pltpu.make_async_remote_copy(
            src_ref=msg.at[k], dst_ref=trx.at[k],
            send_sem=t_send.at[s, k], recv_sem=t_recv.at[s, k],
            device_id={"term": partner_of(k)}, device_id_type=MESH,
        )

    def term_sum(s, msg, trx):
        for k in range(rounds):
            copy = term_copy(s, msg, trx, k)
            copy.start()
            copy.wait()
            msg[k + 1] = msg[k] + trx[k]

    def sq_copy(s, sq, sr, off):
        return pltpu.make_async_remote_copy(
            src_ref=sq, dst_ref=sr.at[me],
            send_sem=s_send.at[s, off], recv_sem=s_recv.at[s, off],
            device_id={"samp": peer_of(off)}, device_id_type=MESH,
        )

    def samp_start(s, sq, sr):
        @pl.loop(1, n_samp)
        def _(off):
            sq_copy(s, sq, sr, off).start()

        sr[me] = sq[...]

    def samp_finish(s, sq, sr):
        @pl.loop(1, n_samp)
        def _(off):
            sq_copy(s, sq, sr, off).wait()

        total = lax.fori_loop(1, n_samp, lambda i, t: t + sr[i], sr[0])
        return lane_sum(total)

    lane = lax.broadcasted_iota(jnp.int32, (num_out, width), 1)

    def pack(values):
        out = jnp.zeros((num_out, width), F32)
        for at, v in enumerate(values):
            out = jnp.where(lane == at, lane_sum(v), out)
        return out

    def pick(block, at):
        return lane_sum(jnp.where(lane == at, block, 0.0))

    def damp_sq(b):
        d = 0.4 * (1.0 + deg[b].astype(F32))
        return d * d

    zero = jnp.zeros((num_out, width), F32)

    adjoint(lambda r: t_ref[:, pl.ds(pl.multiple_of(r * width, width), width)], True)
    pl.semaphore_wait(barrier, n_samp - 1 + rounds)

    def visit0(b, v, carry):
        gs, os = carry
        sq = v * v
        return gs + sq, os + damp_sq(b) * sq

    gs, os = chain(0, acc0, rx0, d0, visit0, (zero, zero))
    forward(d0, msg0)
    msg0[0, rows] = pack([gs, os])
    term_sum(0, msg0, trx0)
    scal = msg0[rounds, rows]
    gsq0, own0 = pick(scal, 0), pick(scal, 1)

    sq = zero
    for r in range(rows):
        v = msg0[rounds, r]
        img0[r] = v
        sq = sq + v * v
    sq0[...] = sq
    samp_start(0, sq0, sr0)
    adjoint(lambda r: img0[r], False)
    chain(1, acc1, rx1, w1, lambda b, v, c: c, 0)
    alpha0 = gsq0 / (samp_finish(0, sq0, sr0) + own0)
    alpha0 = jnp.broadcast_to(alpha0, (num_out, width))

    def make_grad(b, carry):
        ns, s1, s2 = carry
        dd = damp_sq(b)
        d = d0[b]
        g = d - alpha0 * (w1[b] + dd * d)
        g1[b] = g
        dg = dd * g
        return ns + g * g, s1 + dg * g, s2 + dg * d

    ns, s1, s2 = lax.fori_loop(0, terms, make_grad, (zero, zero, zero))
    forward(g1, msg1)
    msg1[0, rows] = pack([ns, s1, s2])
    term_sum(1, msg1, trx1)
    scal = msg1[rounds, rows]
    gsq1, c1, c2 = pick(scal, 0), pick(scal, 1), pick(scal, 2)
    beta = gsq1 / gsq0
    own1 = c1 + 2.0 * beta * c2 + beta * beta * own0
    beta = jnp.broadcast_to(beta, (num_out, width))

    sq = zero
    for r in range(rows):
        v = msg1[rounds, r] + beta * img0[r]
        img1[r] = v
        sq = sq + v * v
    sq1[...] = sq
    samp_start(1, sq1, sr1)
    alpha1 = gsq1 / (samp_finish(1, sq1, sr1) + own1)
    alpha1 = jnp.broadcast_to(alpha1, (num_out, width))
    both = alpha0 + alpha1 * beta

    @pl.loop(0, terms)
    def _(b):
        sol_ref[:, pl.ds(pl.multiple_of(b * width, width), width)] = both * d0[b] + alpha1 * g1[b]

    for r in range(rows):
        cols = slice(r * width, (r + 1) * width)
        res_ref[:, cols] = t_ref[:, cols] - alpha0 * img0[r] - alpha1 * img1[r]

    for k, (acc, rx, d) in enumerate(((acc0, rx0, d0), (acc1, rx1, w1))):
        @pl.loop(0, chunks)
        def _(c):
            to_inner(k, acc, rx, c).wait_send()

            @pl.when(has_outer)
            def _():
                to_outer(k, d, rx, c).wait_send()


def local(n_samp, n_term, blocks, term_index, degrees, targets):
    rows, touched, width = blocks.shape[2], blocks.shape[3], blocks.shape[4]
    terms = degrees.shape[0]
    num_out = targets.shape[0]
    pattern = term_index[0, 0]
    hit = pattern[:, :, None] == jnp.arange(terms, dtype=jnp.int32)
    at = jnp.arange(touched, dtype=jnp.int32)[None, :, None]
    where = jnp.min(jnp.where(hit, at, touched), axis=1)
    where = where + jnp.arange(rows, dtype=jnp.int32)[:, None] * (touched + 1)
    tab = jnp.concatenate([where, pattern], axis=1)

    chunks = min(16, terms)
    rounds = n_term.bit_length() - 1
    blk = (num_out, width)
    vmem = pl.BlockSpec(memory_space=pltpu.VMEM)
    smem = pl.BlockSpec(memory_space=pltpu.SMEM)
    V = pltpu.VMEM
    dma = pltpu.SemaphoreType.DMA
    return pl.pallas_call(
        functools.partial(kernel, n_samp, n_term, chunks),
        out_shape=(
            jax.ShapeDtypeStruct((num_out, terms * width), F32),
            jax.ShapeDtypeStruct((num_out, rows * width), F32),
        ),
        in_specs=[smem, smem, vmem, vmem],
        out_specs=(vmem, vmem),
        scratch_shapes=[
            V((rows, width, touched * width), BF16),
            V((rows, width, touched * width), BF16),
            V((rows * (touched + 1),) + blk, F32),
            V((terms,) + blk, F32),
            V((terms,) + blk, F32),
            V((2, terms) + blk, F32),
            V((2, terms) + blk, F32),
            V((terms,) + blk, F32),
            V((terms,) + blk, F32),
            V((terms,) + blk, F32),
            V((rows,) + blk, F32),
            V((rows,) + blk, F32),
            V((rounds + 1, rows + 1) + blk, F32),
            V((rounds + 1, rows + 1) + blk, F32),
            V((rounds, rows + 1) + blk, F32),
            V((rounds, rows + 1) + blk, F32),
            V((n_samp,) + blk, F32),
            V((n_samp,) + blk, F32),
            V(blk, F32),
            V(blk, F32),
            dma((2, chunks)),
            dma((2, chunks)),
            dma((2, 2, chunks)),
            dma((2, rounds)),
            dma((2, rounds)),
            dma((2, n_samp)),
            dma((2, n_samp)),
        ],
        compiler_params=pltpu.CompilerParams(
            collective_id=0, has_side_effects=True, vmem_limit_bytes=48 * 1024 * 1024,
        ),
    )(tab, degrees, blocks, targets)


def solution(mesh):
    placed = (
        P("samp", "term", "grp", None, None, None),
        P("samp", "term", "grp", None),
        P("term"),
        P("grp", "samp"),
    )
    return jax.shard_map(
        functools.partial(local, mesh.shape["samp"], mesh.shape["term"]),
        mesh=mesh,
        in_specs=placed,
        out_specs=(P("grp", "term"), P("grp", "samp")),
        check_vma=False,
    )
```

time: 247 us -> 259 us (1.049)
  Pallas kernels: 0 us -> 251 us
  waiting for transfers between devices: 152 us -> 0 us
  blocking collectives: 43.2 us -> 0 us
  matrix products: 20.1 us -> 0 us
  between operations: 13.9 us -> 0.65 us
  other arithmetic: 9.76 us -> 1.61 us
  local copies, waits for them, and re-layouts: 8.33 us -> 5.37 us
    pallas_call x0 -> x1, Pallas kernels: none -> 251 us  [local(): pl.pallas_call(functools.partial(kernel, n_samp, n_term, chunks), out_sha...]
    psum x4 -> x0, waiting for transfers between devices: 151 us -> none  [the longest x2 104 us: reduce_adjoint(): return lax.psum(partial_terms, 'samp')]
    psum x5 -> x0, blocking collectives: 43.2 us -> none  [the longest x2 23.4 us: local(): curv_sq = lax.psum(image_sq, 'samp') + damped_total(own_sq)]
    dot_general x8 -> x0, matrix products: 20.1 us -> none  [the longest x2 8.09 us: local(): jnp.einsum('qrnt,rnxt->qrx', picked, design, precision=lax.Precision.HIGH...]
    reduce_sum x5 -> x0, other arithmetic: 5.74 us -> none  [the longest x2 2.14 us: local(): own_sq = jnp.sum(damped * damped, axis=1)]
    unnamed x20 -> x8, local copies, waits for them, and re-layouts: 6.15 us -> 5.37 us
  transfers between devices with their start and end apart: 4 -> 0, of which waited for: 4 -> 0; matrix products, arithmetic and copies ran while one was open for 0% -> 0% of each run, Pallas kernels for 0% -> 0%
where the time goes in v1:
time: 259 us
  Pallas kernels  251 us (97%)
  local copies, waits for them, and re-layouts  5.37 us (2%)
    pallas_call x1, Pallas kernels, local(): pl.pallas_call(functools.partial(kernel, n_samp, n_term, chunks), out_sha...  251 us
    unnamed x8, local copies, waits for them, and re-layouts  5.37 us

profile of v1, /device:TPU:0, one launch (start us, length us, event | category | flops | bytes accessed | tf_op | source)
XLA Modules:
  0.0 258.9 jit_solution(13169048639736324161)
XLA Ops:
  0.6 0.8 select_reduce_fusion
  1.4 0.1 broadcast_add_fusion
  1.5 0.8 pad_add_fusion.tab
  2.3 0.0 copy-start
  2.3 2.2 copy-done
  4.4 0.0 copy-start.1
  4.4 0.9 copy-done.1
  5.3 0.0 copy-start.2
  5.3 0.7 copy-done.2
  6.0 251.3 %shard_map.59 = (f32[32,8192]{1,0:T(8,128)S(1)}, f32[32,1024]{1,0:T(8,128)S(1)}) custom-call(s32[8,72]{1,0:T(8,128)S(1)} %pad_add_fusion.tab, s32[64]{0:T(128)S(1)} %copy-done.2, f32[1,1,8,8,128,128]{5,4,3,2,1,0:T(8,128)S(1)} %copy-done, f32[32,1024]{1,0:T(8,128)S(1)} %copy-done.1), custom_call_target="tpu_custom_call" | custom-call | tf_op jit(solution)/shard_map/pallas_call | solution.py:306
  257.3 1.0 copy.8
  258.2 0.7 copy.9
  (1 shorter events, 0.0 us)
Async XLA Ops:
  2.3 2.2 copy-start
  4.4 0.9 copy-start.1
  5.3 0.7 copy-start.2

commit v2 on v1

--- a/solution.py
+++ b/solution.py
@@ -10,6 +10,7 @@
 MESH = pl.DeviceIdType.MESH
 F32 = jnp.float32
 BF16 = jnp.bfloat16
+LAG = 3
 
 
 def split(x):
@@ -26,7 +27,7 @@
     tab, deg, a_ref, t_ref,
     sol_ref, res_ref,
     ahi, alo, part, acc0, acc1, rx0, rx1, d0, w1, g1,
-    img0, img1, msg0, msg1, trx0, trx1, sr0, sr1, sq0, sq1,
+    img0, img1, msg0, msg1, trx0, trx1, sr0, sr1, sq0, sq1, totals,
     in_send, out_send, chain_recv, t_send, t_recv, s_send, s_recv,
 ):
     rows, touched, width = a_ref.shape[2], a_ref.shape[3], a_ref.shape[4]
@@ -43,7 +44,11 @@
     is_mid = jnp.logical_or(me == half - 1, me == half)
     has_outer = jnp.logical_and(me > 0, me < n_samp - 1)
     outer = jnp.where(low, jnp.maximum(me - 1, 0), jnp.minimum(me + 1, n_samp - 1))
+    away = jnp.where(low, half - 1 - me, me - half)
+    lag = jnp.minimum(LAG * (2 * away + 1), chunks)
     slot_at_inner = jnp.where(is_mid, 1, 0)
+
+    zero = jnp.zeros((num_out, width), F32)
 
     def peer_of(off):
         return lax.rem(me + off, n_samp)
@@ -113,7 +118,7 @@
             device_id={"samp": inner}, device_id_type=MESH,
         ).wait_recv()
 
-    def chain(k, acc, rx, d, visit, carry):
+    def chain(k, acc, rx, d, visit, sums):
         def inbound(c):
             @pl.loop(0, size)
             def _(i):
@@ -130,7 +135,7 @@
 
             to_inner(k, acc, rx, c).start()
 
-        def outbound(c, carry):
+        def outbound(c):
             arrived(k, rx, 1, c)
 
             def one(i, carry):
@@ -140,22 +145,26 @@
                 d[b] = v
                 return visit(b, v, carry)
 
-            carry = lax.fori_loop(0, size, one, carry)
+            carry = lax.fori_loop(0, size, one, tuple(zero for _ in range(sums)))
+            for at, value in enumerate(carry):
+                totals[at] += value
 
             @pl.when(has_outer)
             def _():
                 to_outer(k, d, rx, c).start()
 
-            return carry
-
-        inbound(0)
-
-        def step(c, carry):
-            inbound(c)
-            return outbound(c - 1, carry)
-
-        carry = lax.fori_loop(1, chunks, step, carry)
-        return outbound(chunks - 1, carry)
+        for at in range(sums):
+            totals[at] = zero
+
+        @pl.loop(0, chunks + lag)
+        def _(step):
+            @pl.when(step < chunks)
+            def _():
+                inbound(step)
+
+            @pl.when(step >= lag)
+            def _():
+                outbound(step - lag)
 
     def term_copy(s, msg, trx, k):
         return pltpu.make_async_remote_copy(
@@ -208,8 +217,6 @@
         d = 0.4 * (1.0 + deg[b].astype(F32))
         return d * d
 
-    zero = jnp.zeros((num_out, width), F32)
-
     adjoint(lambda r: t_ref[:, pl.ds(pl.multiple_of(r * width, width), width)], True)
     pl.semaphore_wait(barrier, n_samp - 1 + rounds)
 
@@ -218,9 +225,9 @@
         sq = v * v
         return gs + sq, os + damp_sq(b) * sq
 
-    gs, os = chain(0, acc0, rx0, d0, visit0, (zero, zero))
+    chain(0, acc0, rx0, d0, visit0, 2)
     forward(d0, msg0)
-    msg0[0, rows] = pack([gs, os])
+    msg0[0, rows] = pack([totals[0], totals[1]])
     term_sum(0, msg0, trx0)
     scal = msg0[rounds, rows]
     gsq0, own0 = pick(scal, 0), pick(scal, 1)
@@ -332,6 +339,7 @@
             V((n_samp,) + blk, F32),
             V(blk, F32),
             V(blk, F32),
+            V((2,) + blk, F32),
             dma((2, chunks)),
             dma((2, chunks)),
             dma((2, 2, chunks)),

time: 259 us -> 105 us (0.41)
  Pallas kernels: 251 us -> 96.6 us
    pallas_call x1, Pallas kernels: 251 us -> 96.6 us  [local(): pl.pallas_call(functools.partial(kernel, n_samp, n_term, chunks), out_sha...]
where the time goes in v2:
time: 105 us; the launch traced here: 104 us
  Pallas kernels  96.6 us (92%)
  local copies, waits for them, and re-layouts  5.37 us (5%)
  other arithmetic  1.61 us (2%)
    pallas_call x1, Pallas kernels, local(): pl.pallas_call(functools.partial(kernel, n_samp, n_term, chunks), out_sha...  96.6 us
    unnamed x8, local copies, waits for them, and re-layouts  5.37 us

profile of v2, /device:TPU:0, one launch (start us, length us, event | category | flops | bytes accessed | tf_op | source)
XLA Modules:
  0.0 104.3 jit_solution(10450401883715280740)
XLA Ops:
  0.6 0.8 select_reduce_fusion
  1.4 0.1 broadcast_add_fusion
  1.5 0.8 pad_add_fusion.tab
  2.3 0.0 copy-start
  2.3 2.2 %copy-done = f32[1,1,8,8,128,128]{5,4,3,2,1,0:T(8,128)S(1)} copy-done((f32[1,1,8,8,128,128]{5,4,3,2,1,0:T(8,128)S(1)}, f32[1,1,8,8,128,128]{5,4,3,2,1,0:T(8,128)}, u32[]{:S(2)}) %copy-start) | copy-done | bytes 4194328
  4.4 0.0 copy-start.1
  4.4 0.9 copy-done.1
  5.3 0.0 copy-start.2
  5.3 0.7 copy-done.2
  6.0 96.6 %shard_map.59 = (f32[32,8192]{1,0:T(8,128)S(1)}, f32[32,1024]{1,0:T(8,128)S(1)}) custom-call(s32[8,72]{1,0:T(8,128)S(1)} %pad_add_fusion.tab, s32[64]{0:T(128)S(1)} %copy-done.2, f32[1,1,8,8,128,128]{5,4,3,2,1,0:T(8,128)S(1)} %copy-done, f32[32,1024]{1,0:T(8,128)S(1)} %copy-done.1), custom_call_target="tpu_custom_call" | custom-call | tf_op jit(solution)/shard_map/pallas_call | solution.py:313
  102.6 1.0 copy.8
  103.6 0.7 copy.9
  (1 shorter events, 0.0 us)
Async XLA Ops:
  2.3 2.2 %copy-start = (f32[1,1,8,8,128,128]{5,4,3,2,1,0:T(8,128)S(1)}, f32[1,1,8,8,128,128]{5,4,3,2,1,0:T(8,128)}, u32[]{:S(2)}) copy-start(f32[1,1,8,8,128,128]{5,4,3,2,1,0:T(8,128)} %a_ref.1) | copy-start | bytes 12582916
  4.4 0.9 copy-start.1
  5.3 0.7 copy-start.2

commit v3 on v2

--- a/solution.py
+++ b/solution.py
@@ -10,7 +10,9 @@
 MESH = pl.DeviceIdType.MESH
 F32 = jnp.float32
 BF16 = jnp.bfloat16
-LAG = 3
+LAG = 4
+LAG_MID = 2
+PIECES = 3
 
 
 def split(x):
@@ -24,18 +26,19 @@
 
 def kernel(
     n_samp, n_term, chunks,
-    tab, deg, a_ref, t_ref,
+    idx_ref, deg, a_hbm, t_ref,
     sol_ref, res_ref,
-    ahi, alo, part, acc0, acc1, rx0, rx1, d0, w1, g1,
+    tab, tab_v, tab_sem, a_ref, a_sem, ahi, alo, part, acc0, acc1, rx0, rx1, d0, w1, g1,
     img0, img1, msg0, msg1, trx0, trx1, sr0, sr1, sq0, sq1, totals,
     in_send, out_send, chain_recv, t_send, t_recv, s_send, s_recv,
 ):
-    rows, touched, width = a_ref.shape[2], a_ref.shape[3], a_ref.shape[4]
+    rows, touched, width = a_ref.shape[0], a_ref.shape[1], a_ref.shape[2]
     num_out = t_ref.shape[0]
     terms = deg.shape[0]
     size = terms // chunks
     half = n_samp // 2
     rounds = n_term.bit_length() - 1
+    cuts = [(rows + 1) * p // PIECES for p in range(PIECES + 1)]
     me = lax.axis_index("samp")
     tm = lax.axis_index("term")
 
@@ -45,7 +48,7 @@
     has_outer = jnp.logical_and(me > 0, me < n_samp - 1)
     outer = jnp.where(low, jnp.maximum(me - 1, 0), jnp.minimum(me + 1, n_samp - 1))
     away = jnp.where(low, half - 1 - me, me - half)
-    lag = jnp.minimum(LAG * (2 * away + 1), chunks)
+    lag = jnp.minimum(LAG * 2 * away + LAG_MID, chunks)
     slot_at_inner = jnp.where(is_mid, 1, 0)
 
     zero = jnp.zeros((num_out, width), F32)
@@ -57,6 +60,13 @@
         step = 2 ** k
         return tm + (1 - 2 * lax.rem(tm // step, 2)) * step
 
+    def block_copy(r):
+        return pltpu.make_async_copy(a_hbm.at[0, 0, r], a_ref.at[r], a_sem.at[r])
+
+    @pl.loop(0, rows)
+    def _(r):
+        block_copy(r).start()
+
     barrier = pltpu.get_barrier_semaphore()
 
     @pl.loop(1, n_samp)
@@ -65,13 +75,27 @@
 
     for k in range(rounds):
         pl.semaphore_signal(barrier, inc=1, device_id={"term": partner_of(k)}, device_id_type=MESH)
+
+    pattern = idx_ref[0, 0]
+    shape = tab_v.shape
+    term = lax.broadcasted_iota(jnp.int32, shape, 1)
+    none = lax.broadcasted_iota(jnp.int32, shape, 0) * (touched + 1) + touched
+    table = none
+    for n in range(touched):
+        col = pattern[:, n:n + 1]
+        table = jnp.where(term == col, none + (n - touched), table)
+        table = jnp.where(term == terms + n, col, table)
+    tab_v[...] = table
+    tab_copy = pltpu.make_async_copy(tab_v, tab, tab_sem)
+    tab_copy.start()
 
     def adjoint(load, first):
         @pl.loop(0, rows)
         def _(r):
             if first:
+                block_copy(r).wait()
                 for n in range(touched):
-                    hi, lo = split(a_ref[0, 0, r, n])
+                    hi, lo = split(a_ref[r, n])
                     ahi[r, :, n * width:(n + 1) * width] = hi
                     alo[r, :, n * width:(n + 1) * width] = lo
                 part[r * (touched + 1) + touched] = jnp.zeros((num_out, width), F32)
@@ -83,8 +107,8 @@
                 q = jnp.dot(hi, alo[r, :, cols], preferred_element_type=F32)
                 part[r * (touched + 1) + n] = p[:num_out] + p[num_out:] + q
 
-    def forward(src, dst):
-        @pl.loop(0, rows)
+    def forward(src, dst, start, stop):
+        @pl.loop(start, stop)
         def _(r):
             x = jnp.concatenate([src[tab[r, terms + n]] for n in range(touched)], axis=1)
             hi, lo = split(x)
@@ -120,7 +144,7 @@
 
     def chain(k, acc, rx, d, visit, sums):
         def inbound(c):
-            @pl.loop(0, size)
+            @pl.loop(0, size, unroll=True)
             def _(i):
                 b = c * size + i
                 total = part[tab[0, b]]
@@ -145,7 +169,7 @@
                 d[b] = v
                 return visit(b, v, carry)
 
-            carry = lax.fori_loop(0, size, one, tuple(zero for _ in range(sums)))
+            carry = lax.fori_loop(0, size, one, tuple(zero for _ in range(sums)), unroll=True)
             for at, value in enumerate(carry):
                 totals[at] += value
 
@@ -166,19 +190,32 @@
             def _():
                 outbound(step - lag)
 
-    def term_copy(s, msg, trx, k):
+    def term_copy(s, msg, trx, k, p):
+        part_of = pl.ds(cuts[p], cuts[p + 1] - cuts[p])
         return pltpu.make_async_remote_copy(
-            src_ref=msg.at[k], dst_ref=trx.at[k],
-            send_sem=t_send.at[s, k], recv_sem=t_recv.at[s, k],
+            src_ref=msg.at[k, part_of], dst_ref=trx.at[k, part_of],
+            send_sem=t_send.at[s, k, p], recv_sem=t_recv.at[s, k, p],
             device_id={"term": partner_of(k)}, device_id_type=MESH,
         )
 
-    def term_sum(s, msg, trx):
-        for k in range(rounds):
-            copy = term_copy(s, msg, trx, k)
-            copy.start()
-            copy.wait()
-            msg[k + 1] = msg[k] + trx[k]
+    def image_sum(s, src, msg, trx, scalars):
+        def advance(k, p):
+            term_copy(s, msg, trx, k, p).wait()
+            part_of = pl.ds(cuts[p], cuts[p + 1] - cuts[p])
+            msg[k + 1, part_of] = msg[k, part_of] + trx[k, part_of]
+            if k + 1 < rounds:
+                term_copy(s, msg, trx, k + 1, p).start()
+
+        msg[0, rows] = pack(scalars)
+        for p in range(PIECES):
+            forward(src, msg, cuts[p], min(cuts[p + 1], rows))
+            term_copy(s, msg, trx, 0, p).start()
+            if p:
+                advance(0, p - 1)
+        advance(0, PIECES - 1)
+        for k in range(1, rounds):
+            for p in range(PIECES):
+                advance(k, p)
 
     def sq_copy(s, sq, sr, off):
         return pltpu.make_async_remote_copy(
@@ -218,6 +255,7 @@
         return d * d
 
     adjoint(lambda r: t_ref[:, pl.ds(pl.multiple_of(r * width, width), width)], True)
+    tab_copy.wait()
     pl.semaphore_wait(barrier, n_samp - 1 + rounds)
 
     def visit0(b, v, carry):
@@ -226,9 +264,7 @@
         return gs + sq, os + damp_sq(b) * sq
 
     chain(0, acc0, rx0, d0, visit0, 2)
-    forward(d0, msg0)
-    msg0[0, rows] = pack([totals[0], totals[1]])
-    term_sum(0, msg0, trx0)
+    image_sum(0, d0, msg0, trx0, [totals[0], totals[1]])
     scal = msg0[rounds, rows]
     gsq0, own0 = pick(scal, 0), pick(scal, 1)
 
@@ -253,10 +289,8 @@
         dg = dd * g
         return ns + g * g, s1 + dg * g, s2 + dg * d
 
-    ns, s1, s2 = lax.fori_loop(0, terms, make_grad, (zero, zero, zero))
-    forward(g1, msg1)
-    msg1[0, rows] = pack([ns, s1, s2])
-    term_sum(1, msg1, trx1)
+    ns, s1, s2 = lax.fori_loop(0, terms, make_grad, (zero, zero, zero), unroll=4)
+    image_sum(1, g1, msg1, trx1, [ns, s1, s2])
     scal = msg1[rounds, rows]
     gsq1, c1, c2 = pick(scal, 0), pick(scal, 1), pick(scal, 2)
     beta = gsq1 / gsq0
@@ -274,7 +308,7 @@
     alpha1 = jnp.broadcast_to(alpha1, (num_out, width))
     both = alpha0 + alpha1 * beta
 
-    @pl.loop(0, terms)
+    @pl.loop(0, terms, unroll=4)
     def _(b):
         sol_ref[:, pl.ds(pl.multiple_of(b * width, width), width)] = both * d0[b] + alpha1 * g1[b]
 
@@ -296,16 +330,10 @@
     rows, touched, width = blocks.shape[2], blocks.shape[3], blocks.shape[4]
     terms = degrees.shape[0]
     num_out = targets.shape[0]
-    pattern = term_index[0, 0]
-    hit = pattern[:, :, None] == jnp.arange(terms, dtype=jnp.int32)
-    at = jnp.arange(touched, dtype=jnp.int32)[None, :, None]
-    where = jnp.min(jnp.where(hit, at, touched), axis=1)
-    where = where + jnp.arange(rows, dtype=jnp.int32)[:, None] * (touched + 1)
-    tab = jnp.concatenate([where, pattern], axis=1)
-
     chunks = min(16, terms)
     rounds = n_term.bit_length() - 1
     blk = (num_out, width)
+    tab_cols = -(-(terms + touched) // 128) * 128
     vmem = pl.BlockSpec(memory_space=pltpu.VMEM)
     smem = pl.BlockSpec(memory_space=pltpu.SMEM)
     V = pltpu.VMEM
@@ -316,9 +344,14 @@
             jax.ShapeDtypeStruct((num_out, terms * width), F32),
             jax.ShapeDtypeStruct((num_out, rows * width), F32),
         ),
-        in_specs=[smem, smem, vmem, vmem],
+        in_specs=[vmem, smem, pl.BlockSpec(memory_space=pltpu.HBM), vmem],
         out_specs=(vmem, vmem),
         scratch_shapes=[
+            pltpu.SMEM((rows, tab_cols), jnp.int32),
+            V((rows, tab_cols), jnp.int32),
+            dma,
+            V((rows, touched, width, width), F32),
+            dma((rows,)),
             V((rows, width, touched * width), BF16),
             V((rows, width, touched * width), BF16),
             V((rows * (touched + 1),) + blk, F32),
@@ -343,15 +376,15 @@
             dma((2, chunks)),
             dma((2, chunks)),
             dma((2, 2, chunks)),
-            dma((2, rounds)),
-            dma((2, rounds)),
+            dma((2, rounds, PIECES)),
+            dma((2, rounds, PIECES)),
             dma((2, n_samp)),
             dma((2, n_samp)),
         ],
         compiler_params=pltpu.CompilerParams(
             collective_id=0, has_side_effects=True, vmem_limit_bytes=48 * 1024 * 1024,
         ),
-    )(tab, degrees, blocks, targets)
+    )(term_index, degrees, blocks, targets)
 
 
 def solution(mesh):

time: 105 us -> 98.5 us (0.938)
  Pallas kernels: 96.6 us -> 91.6 us
  other arithmetic: 1.61 us -> 0 us
    pallas_call x1, Pallas kernels: 96.6 us -> 91.6 us  [local(): pl.pallas_call(functools.partial(kernel, n_samp, n_term, chunks), out_sha...]
    unnamed x8 -> x10, local copies, waits for them, and re-layouts: 5.37 us -> 6.05 us
where the time goes in v3:
time: 98.5 us; the launch traced here: 98.3 us
  Pallas kernels  91.6 us (93%)
  local copies, waits for them, and re-layouts  6.05 us (6%)
    pallas_call x1, Pallas kernels, local(): pl.pallas_call(functools.partial(kernel, n_samp, n_term, chunks), out_sha...  91.6 us
    unnamed x10, local copies, waits for them, and re-layouts  6.05 us

profile of v3, /device:TPU:0, one launch (start us, length us, event | category | flops | bytes accessed | tf_op | source)
XLA Modules:
  0.0 98.3 jit_solution(12726711052137163123)
XLA Ops:
  0.6 0.0 copy-start
  0.6 2.2 %copy-done = f32[1,1,8,8,128,128]{5,4,3,2,1,0:T(8,128)S(1)} copy-done((f32[1,1,8,8,128,128]{5,4,3,2,1,0:T(8,128)S(1)}, f32[1,1,8,8,128,128]{5,4,3,2,1,0:T(8,128)}, u32[]{:S(2)}) %copy-start) | copy-done | bytes 4194328
  2.8 0.0 copy-start.1
  2.8 0.9 copy-done.1
  3.7 0.0 copy-start.2
  3.7 0.7 copy-done.2
  4.4 0.0 copy-start.3
  4.4 0.7 copy-done.3
  5.1 91.6 %shard_map.59 = (f32[32,8192]{1,0:T(8,128)S(1)}, f32[32,1024]{1,0:T(8,128)S(1)}) custom-call(s32[1,1,8,8]{3,2,1,0:T(8,128)S(1)} %copy-done.2, s32[64]{0:T(128)S(1)} %copy-done.3, f32[1,1,8,8,128,128]{5,4,3,2,1,0:T(8,128)S(1)} %copy-done, f32[32,1024]{1,0:T(8,128)S(1)} %copy-done.1), custom_call_target="tpu_custom_call" | custom-call | tf_op jit(solution)/shard_map/pallas_call | solution.py:341
  96.7 1.0 copy.8
  97.6 0.7 copy.9
Async XLA Ops:
  0.6 2.2 %copy-start = (f32[1,1,8,8,128,128]{5,4,3,2,1,0:T(8,128)S(1)}, f32[1,1,8,8,128,128]{5,4,3,2,1,0:T(8,128)}, u32[]{:S(2)}) copy-start(f32[1,1,8,8,128,128]{5,4,3,2,1,0:T(8,128)} %a_hbm.1) | copy-start | bytes 12582916
  2.8 0.9 copy-start.1
  3.7 0.7 copy-start.2
  4.4 0.7 copy-start.3

commit v4 on v3

--- a/solution.py
+++ b/solution.py
@@ -90,7 +90,7 @@
     tab_copy.start()
 
     def adjoint(load, first):
-        @pl.loop(0, rows)
+        @pl.loop(0, rows, unroll=2)
         def _(r):
             if first:
                 block_copy(r).wait()
@@ -108,7 +108,7 @@
                 part[r * (touched + 1) + n] = p[:num_out] + p[num_out:] + q
 
     def forward(src, dst, start, stop):
-        @pl.loop(start, stop)
+        @pl.loop(start, stop, unroll=True)
         def _(r):
             x = jnp.concatenate([src[tab[r, terms + n]] for n in range(touched)], axis=1)
             hi, lo = split(x)
@@ -162,20 +162,23 @@
         def outbound(c):
             arrived(k, rx, 1, c)
 
+            @pl.loop(0, size, unroll=True)
+            def _(i):
+                b = c * size + i
+                got = rx[1, b]
+                d[b] = jnp.where(is_mid, got + acc[b], got)
+
+            @pl.when(has_outer)
+            def _():
+                to_outer(k, d, rx, c).start()
+
             def one(i, carry):
                 b = c * size + i
-                got = rx[1, b]
-                v = jnp.where(is_mid, got + acc[b], got)
-                d[b] = v
-                return visit(b, v, carry)
+                return visit(b, d[b], carry)
 
             carry = lax.fori_loop(0, size, one, tuple(zero for _ in range(sums)), unroll=True)
             for at, value in enumerate(carry):
                 totals[at] += value
-
-            @pl.when(has_outer)
-            def _():
-                to_outer(k, d, rx, c).start()
 
         for at in range(sums):
             totals[at] = zero

time: 98.5 us -> 97.9 us (level)
  no operation moved by 1% of the time
where the time goes in v4:
time: 97.9 us; the launch traced here: 97.7 us
  Pallas kernels  91 us (93%)
  local copies, waits for them, and re-layouts  6.05 us (6%)
    pallas_call x1, Pallas kernels, local(): pl.pallas_call(functools.partial(kernel, n_samp, n_term, chunks), out_sha...  91 us
    unnamed x10, local copies, waits for them, and re-layouts  6.05 us

profile of v4, /device:TPU:0, one launch (start us, length us, event | category | flops | bytes accessed | tf_op | source)
XLA Modules:
  0.0 97.7 jit_solution(9003908477639237414)
XLA Ops:
  0.6 0.0 copy-start
  0.6 2.2 %copy-done = f32[1,1,8,8,128,128]{5,4,3,2,1,0:T(8,128)S(1)} copy-done((f32[1,1,8,8,128,128]{5,4,3,2,1,0:T(8,128)S(1)}, f32[1,1,8,8,128,128]{5,4,3,2,1,0:T(8,128)}, u32[]{:S(2)}) %copy-start) | copy-done | bytes 4194328
  2.8 0.0 copy-start.1
  2.8 0.9 copy-done.1
  3.7 0.0 copy-start.2
  3.7 0.7 copy-done.2
  4.4 0.0 copy-start.3
  4.4 0.7 copy-done.3
  5.1 91.0 %shard_map.59 = (f32[32,8192]{1,0:T(8,128)S(1)}, f32[32,1024]{1,0:T(8,128)S(1)}) custom-call(s32[1,1,8,8]{3,2,1,0:T(8,128)S(1)} %copy-done.2, s32[64]{0:T(128)S(1)} %copy-done.3, f32[1,1,8,8,128,128]{5,4,3,2,1,0:T(8,128)S(1)} %copy-done, f32[32,1024]{1,0:T(8,128)S(1)} %copy-done.1), custom_call_target="tpu_custom_call" | custom-call | tf_op jit(solution)/shard_map/pallas_call | solution.py:344
  96.1 1.0 copy.8
  97.0 0.7 copy.9
Async XLA Ops:
  0.6 2.2 %copy-start = (f32[1,1,8,8,128,128]{5,4,3,2,1,0:T(8,128)S(1)}, f32[1,1,8,8,128,128]{5,4,3,2,1,0:T(8,128)}, u32[]{:S(2)}) copy-start(f32[1,1,8,8,128,128]{5,4,3,2,1,0:T(8,128)} %a_hbm.1) | copy-start | bytes 12582916
  2.8 0.9 copy-start.1
  3.7 0.7 copy-start.2
  4.4 0.7 copy-start.3
